TPU v7x, 32 devices: a whole 2x2x4 slice. The times are simulated.
32 devices in a mesh: row: 16 (over z, x, core), col: 2 (over y).
Axes of the slice: x: 2, y: 2, z: 4, core: 2. Of those that a mesh axis runs over, the one named last changes fastest.
Arguments:
- pair: bfloat16 [512, 512, 128], P('row', 'col'), may hold values from -6 to 6
- cotangent: bfloat16 [64, 512, 512], P(None, 'row', 'col'), may hold values from -0.59765625 to 0.59765625
- w_left: bfloat16 [128, 64], replicated, may hold values from -0.5 to 0.5
- w_left_gate: bfloat16 [128, 64], replicated, may hold values from -0.5 to 0.5
- w_right: bfloat16 [128, 64], replicated, may hold values from -0.5 to 0.5
- w_right_gate: bfloat16 [128, 64], replicated, may hold values from -0.5 to 0.5
Outputs:
- pair_gradient: bfloat16 [512, 512, 128], P('row', 'col')
- grad_left: float32 [128, 64], replicated
- grad_left_gate: float32 [128, 64], replicated
- grad_right: float32 [128, 64], replicated
- grad_right_gate: float32 [128, 64], replicated
All inputs are finite; a program needn't handle non-finite values.
Results may differ from a plain program's by a relative error of at most 0.0082.
Values may be sent and summed in bfloat16 or wider, within the bound.
No kernel may reach another device: no remote copies, remote signals or barrier semaphores. Data moves between devices by JAX's collectives and lax.ppermute only.
A program may use at most 128 MiB of HBM per device.

v0:
```python
import jax
import jax.numpy as jnp
from jax import lax
from jax.sharding import PartitionSpec as P


def shards(pair, cotangent, w_left, w_left_gate, w_right, w_right_gate):
    pair_f = pair.astype(jnp.float32)
    average = jnp.mean(pair_f, axis=-1, keepdims=True)
    centered_input = pair_f - average
    variance = jnp.mean(centered_input * centered_input, axis=-1, keepdims=True)
    inverse_scale = 1.0 / jnp.sqrt(variance + 1e-05)
    standardized_input = centered_input * inverse_scale
    normalized_input = standardized_input.astype(jnp.bfloat16)
    stacked = jnp.concatenate([w_left, w_left_gate, w_right, w_right_gate], axis=1)
    projected = jnp.einsum(
        "rcd,dh->hrc", normalized_input, stacked, preferred_element_type=jnp.float32
    )
    q_left, p_left, q_right, p_right = jnp.split(projected, 4, axis=0)
    s_left = jax.nn.sigmoid(p_left)
    s_right = jax.nn.sigmoid(p_right)
    left = (s_left * q_left).astype(jnp.bfloat16)
    right = (s_right * q_right).astype(jnp.bfloat16)
    g_chan, left_chan, right_chan = (
        lax.all_to_all(cotangent, "col", split_axis=0, concat_axis=2, tiled=True),
        lax.all_to_all(left, "col", split_axis=0, concat_axis=2, tiled=True),
        lax.all_to_all(right, "col", split_axis=0, concat_axis=2, tiled=True),
    )
    residues = g_chan.shape[2]
    g_columns = lax.all_to_all(g_chan, "row", split_axis=2, concat_axis=1, tiled=True)
    d_left = jnp.einsum(
        "hij,hjk->hik",
        g_chan,
        lax.all_gather(right_chan, "row", axis=1, tiled=True),
        preferred_element_type=jnp.float32,
    )
    d_right = jnp.einsum(
        "hij,hik->hjk",
        g_columns,
        lax.all_gather(left_chan, "row", axis=1, tiled=True),
        preferred_element_type=jnp.float32,
    )
    d_left_tile, d_right_tile = (
        lax.all_to_all(d_left.astype(jnp.bfloat16), "col", split_axis=2, concat_axis=0, tiled=True),
        lax.all_to_all(
            d_right.astype(jnp.bfloat16), "col", split_axis=2, concat_axis=0, tiled=True
        ),
    )
    grad_l = d_left_tile.astype(jnp.float32)
    grad_r = d_right_tile.astype(jnp.float32)
    e_left = grad_l * s_left
    f_left = grad_l * q_left * s_left * (1.0 - s_left)
    e_right = grad_r * s_right
    f_right = grad_r * q_right * s_right * (1.0 - s_right)
    grads = jnp.concatenate([e_left, f_left, e_right, f_right], axis=0).astype(jnp.bfloat16)
    local_weights = jnp.einsum(
        "rcd,hrc->dh", normalized_input, grads, preferred_element_type=jnp.float32
    )
    total_weights = lax.psum(local_weights, ("row", "col")) / residues
    normalized_gradient = jnp.einsum(
        "hrc,dh->rcd", grads, stacked, preferred_element_type=jnp.float32
    )
    gradient_mean = jnp.mean(normalized_gradient, axis=-1, keepdims=True)
    gradient_input_mean = jnp.mean(normalized_gradient * standardized_input, axis=-1, keepdims=True)
    pair_gradient = (
        (normalized_gradient - gradient_mean - standardized_input * gradient_input_mean)
        * inverse_scale
    ).astype(jnp.bfloat16)
    pieces_w = jnp.split(total_weights, 4, axis=1)
    return (pair_gradient, pieces_w[0], pieces_w[1], pieces_w[2], pieces_w[3])


def solution(mesh):
    in_specs = (P("row", "col", None), P(None, "row", "col"), P(), P(), P(), P())
    out_specs = (P("row", "col", None), P(), P(), P(), P())
    return jax.shard_map(shards, mesh=mesh, in_specs=in_specs, out_specs=out_specs, check_vma=False)
```

profile of v0, /device:TPU:0, one launch (start us, length us, event | category | flops | bytes accessed | tf_op | source)
XLA Modules:
  0.0 582.6 jit_solution(16603435236060173384)
XLA Ops:
  7.3 3.3 copy.25
  10.9 0.7 fusion.9
  11.7 1.3 fusion.26
  13.0 0.6 multiply_convert_fusion.1
  13.6 0.6 copy.27
  14.2 17.6 %all_to_all.90 = bf16[64,32,256]{2,1,0:T(8,128)(2,1)S(1)} all-to-all(bf16[64,32,256]{2,1,0:T(8,128)(2,1)S(1)} %copy.27), channel_id=1, replica_groups=mesh['row'=16,'col'=2] {'col'}, dimensions={0} | all-to-all | bytes 2097152 | tf_op jit(solution)/shard_map/all_to_all | solution.py:27
  31.8 1.1 copy.54
  32.9 1.5 all_to_all.69
  34.5 16.4 %all_to_all.91 = bf16[64,32,256]{2,1,0:T(8,128)(2,1)S(1)} all-to-all(bf16[64,32,256]{2,1,0:T(8,128)(2,1)} %param.7), channel_id=1, replica_groups=mesh['row'=16,'col'=2] {'col'}, dimensions={0} | all-to-all | bytes 2097152 | tf_op jit(solution)/shard_map/all_to_all | solution.py:25
  50.9 2.1 copy.53
  53.0 1.7 all_to_all.73
  54.7 107.2 %all-gather.3.cloned.1.call-done = bf16[32,512,512]{2,1,0:T(8,128)(2,1)} async-done(((bf16[32,32,512]{2,1,0:T(8,128)(2,1)}), bf16[32,512,512]{2,1,0:T(8,128)(2,1)}) %all-gather.3.cloned.1.call-update) | async-done | bytes 16777232 | tf_op jit(solution)/shard_map/all_gather | solution.py:34
  161.9 9.6 %fusion.28 = bf16[32,32,512]{2,1,0:T(8,128)(2,1)} fusion(bf16[32,32,512]{2,1,0:T(8,128)(2,1)S(1)} %all_to_all.73, bf16[32,512,512]{2,1,0:T(8,128)(2,1)} %all-gather.3.cloned.1.call-done), kind=kOutput, calls=%fused_computation.40 | convolution fusion | flops 537395200 | bytes 18874368 | tf_op jit(solution)/shard_map/hij,hjk->hik/dot_general | solution.py:31
  171.5 7.2 %copy.30 = bf16[32,32,512]{1,0,2:T(8,128)(2,1)} copy(bf16[32,32,512]{2,1,0:T(8,128)(2,1)} %fusion.28) | data formatting | bytes 2097152 | tf_op jit(solution)/shard_map/convert_element_type | solution.py:44
  178.7 6.5 %reshape.50 = bf16[2,2,131072]{2,1,0:T(2,128)(2,1)} reshape(bf16[512,32,32]{2,1,0:T(8,128)(2,1)} %bitcast.73) | data formatting | bytes 2097152
  185.2 18.7 %all_to_all.92 = bf16[2,2,131072]{2,1,0:T(2,128)(2,1)} all-to-all(bf16[2,2,131072]{2,1,0:T(2,128)(2,1)} %reshape.50), channel_id=1, replica_groups=mesh['row'=16,'col'=2] {'col'}, dimensions={0} | all-to-all | bytes 2097152 | tf_op jit(solution)/shard_map/all_to_all | solution.py:44
  203.9 4.6 reshape.51
  208.5 7.1 %copy.31 = f32[32,32,2,256]{3,0,2,1:T(8,128)} copy(bf16[32,32,2,256]{1,0,3,2:T(8,128)(2,1)} %bitcast.74) | data formatting | bytes 3145728 | tf_op jit(solution)/shard_map/convert_element_type | solution.py:49
  215.6 5.2 fusion.20
  220.8 0.6 copy.32
  221.4 15.9 %all_to_all.93 = bf16[64,32,256]{2,1,0:T(8,128)(2,1)S(1)} all-to-all(bf16[64,32,256]{2,1,0:T(8,128)(2,1)S(1)} %copy.32), channel_id=1, replica_groups=mesh['row'=16,'col'=2] {'col'}, dimensions={0} | all-to-all | bytes 2097152 | tf_op jit(solution)/shard_map/all_to_all | solution.py:26
  237.3 2.1 copy.52
  239.3 2.5 all_to_all.78
  242.1 6.5 %copy.34 = bf16[32,32,512]{1,0,2:T(8,128)(2,1)} copy(bf16[32,32,512]{2,1,0:T(8,128)(2,1)S(1)} %all_to_all.73) | data formatting | bytes 2097152 | tf_op jit(solution)/shard_map/all_to_all | solution.py:25
  248.6 6.8 %reshape.46 = bf16[16,2,16384]{2,1,0:T(2,128)(2,1)S(1)} reshape(bf16[512,32,32]{2,1,0:T(8,128)(2,1)} %bitcast.75) | data formatting | bytes 2097152
  255.4 48.9 %all_to_all.94 = bf16[16,2,16384]{2,1,0:T(2,128)(2,1)} all-to-all(bf16[16,2,16384]{2,1,0:T(2,128)(2,1)S(1)} %reshape.46), channel_id=1, replica_groups=mesh['row'=16,'col'=2] {'row'}, dimensions={0} | all-to-all | bytes 2097152 | tf_op jit(solution)/shard_map/all_to_all | solution.py:30
  304.3 6.5 %reshape.47 = bf16[512,32,32]{2,1,0:T(8,128)(2,1)} reshape(bf16[16,2,16384]{2,1,0:T(2,128)(2,1)} %all_to_all.94) | data formatting | bytes 2097152
  310.8 6.9 %copy.51 = bf16[32,32,16,32]{1,2,3,0:T(8,128)(2,1)} copy(bf16[32,32,16,32]{1,0,3,2:T(8,128)(2,1)} %bitcast.78) | data formatting | bytes 2097152 | tf_op jit(solution)/shard_map/all_to_all | solution.py:30
  317.7 5.9 %all_to_all.82 = bf16[32,512,32]{1,2,0:T(8,128)(2,1)S(1)} reshape(bf16[32,16,32,32]{2,1,3,0:T(8,128)(2,1)} %bitcast.79) | data formatting | bytes 2097152 | tf_op jit(solution)/shard_map/all_to_all | solution.py:30
  323.6 64.9 %all-gather.5.cloned.1.call-done = bf16[32,512,512]{2,1,0:T(8,128)(2,1)} async-done(((bf16[32,32,512]{2,1,0:T(8,128)(2,1)}), bf16[32,512,512]{2,1,0:T(8,128)(2,1)}) %all-gather.5.cloned.1.call-update) | async-done | bytes 16777232 | tf_op jit(solution)/shard_map/all_gather | solution.py:40
  388.5 9.6 %fusion.29 = bf16[32,32,512]{2,1,0:T(8,128)(2,1)} fusion(bf16[32,512,32]{1,2,0:T(8,128)(2,1)S(1)} %all_to_all.82, bf16[32,512,512]{2,1,0:T(8,128)(2,1)} %all-gather.5.cloned.1.call-done), kind=kOutput, calls=%fused_computation.41 | convolution fusion | flops 537395200 | bytes 18874368 | tf_op jit(solution)/shard_map/hij,hik->hjk/dot_general | solution.py:37
  398.1 7.2 %copy.36 = bf16[32,32,512]{1,0,2:T(8,128)(2,1)} copy(bf16[32,32,512]{2,1,0:T(8,128)(2,1)} %fusion.29) | data formatting | bytes 2097152 | tf_op jit(solution)/shard_map/convert_element_type | solution.py:46
  405.3 5.7 reshape.48
  411.0 17.8 %all_to_all.95 = bf16[2,2,131072]{2,1,0:T(2,128)(2,1)} all-to-all(bf16[2,2,131072]{2,1,0:T(2,128)(2,1)S(1)} %reshape.48), channel_id=1, replica_groups=mesh['row'=16,'col'=2] {'col'}, dimensions={0} | all-to-all | bytes 2097152 | tf_op jit(solution)/shard_map/all_to_all | solution.py:45
  428.8 4.6 reshape.49
  433.3 7.1 %copy.37 = f32[32,32,2,256]{3,0,2,1:T(8,128)} copy(bf16[32,32,2,256]{1,0,3,2:T(8,128)(2,1)} %bitcast.77) | data formatting | bytes 3145728 | tf_op jit(solution)/shard_map/convert_element_type | solution.py:50
  440.4 4.0 fusion.16
  444.4 0.9 copy-done.3
  445.7 2.2 fusion.30
  447.9 4.1 fusion.37
  452.0 5.0 fusion.8
  457.0 4.1 copy.39
  461.0 110.8 %all-reduce.2.cloned.1.call-done = f32[128,256]{1,0:T(8,128)} async-done(((f32[128,256]{1,0:T(8,128)}), f32[128,256]{1,0:T(8,128)}) %all-reduce.2.cloned.1.call-update) | async-done | bytes 131088 | tf_op jit(solution)/shard_map/psum | solution.py:59
  571.8 0.9 broadcast_multiply_fusion
  572.8 0.7 copy.43
  573.5 0.7 copy.42
  574.2 0.7 copy.41
  574.9 0.7 copy.40
  (28 shorter events, 1.3 us)
Async XLA Ops:
  7.2 4.5 copy-start.5
  7.2 4.5 copy-start.6
  7.2 4.5 copy-start.7
  7.2 4.5 copy-start.8
  7.2 154.7 %all-gather.3.cloned.1.call-start = ((), (), s32[]{:S(2)}) async-start(), calls=%async_computation.6 | async-start | bytes 17825792 | tf_op jit(solution)/shard_map/all_gather | solution.py:34
  12.9 18.8 %copy-start = (f32[256,32,256]{2,0,1:T(8,128)}, f32[256,32,256]{2,0,1:T(8,128)S(1)}, u32[]{:S(2)}) copy-start(f32[256,32,256]{2,0,1:T(8,128)S(1)} %fusion.26) | copy-start | bytes 25165828
  34.4 354.0 %all-gather.5.cloned.1.call-start = ((), (), s32[]{:S(2)}) async-start(), calls=%async_computation.7 | async-start | bytes 17825792 | tf_op jit(solution)/shard_map/all_gather | solution.py:40
  241.9 329.9 %all-reduce.2.cloned.1.call-start = ((), (), s32[]{:S(2)}) async-start(), calls=%async_computation.8 | async-start | bytes 262144 | tf_op jit(solution)/shard_map/psum | solution.py:59
  440.4 5.3 copy-start.1
  440.4 5.3 copy-start.2
  444.4 1.0 copy-start.3
  444.4 1.3 copy-start.4
Sparse Core Ops, SparseCore 0:
  34.6 127.3 all-gather.2
  242.0 146.4 all-gather.4
  452.1 119.6 all-reduce.1
where the time goes:
time: 587 us; the launch traced here: 583 us
  waiting for transfers between devices  283 us (48%)
  blocking collectives  135 us (23%)
  local copies, waits for them, and re-layouts  106 us (18%)
  matrix products  26.8 us (5%)
  other arithmetic  16.7 us (3%)
  between operations  14.4 us (2%)
    psum x1, waiting for transfers between devices, shards(): total_weights = lax.psum(local_weights, ('row', 'col')) / residues  111 us
    all_gather x1, waiting for transfers between devices, shards(): lax.all_gather(right_chan, 'row', axis=1, tiled=True)  107 us
    all_gather x1, waiting for transfers between devices, shards(): lax.all_gather(left_chan, 'row', axis=1, tiled=True)  64.9 us
    all_to_all x1, blocking collectives, shards(): lax.all_to_all(g_chan, 'row', split_axis=2, concat_axis=1, tiled=True)  48.9 us
    unnamed x30, local copies, waits for them, and re-layouts  46 us
    all_to_all x1, blocking collectives, shards(): lax.all_to_all(d_left.astype(jnp.bfloat16), 'col', split_axis=2, concat_a...  18.7 us
    all_to_all x1, blocking collectives, shards(): lax.all_to_all(d_right.astype(jnp.bfloat16), 'col', split_axis=2, concat_...  17.8 us
    all_to_all x1, blocking collectives, shards(): lax.all_to_all(right, 'col', split_axis=0, concat_axis=2, tiled=True)  17.6 us
  transfers between devices with their start and end apart: 3, of which 3 were waited for; matrix products, arithmetic and copies ran while one was open for 6% of the time, Pallas kernels for 0%

commit v1 on v0

--- a/solution.py
+++ b/solution.py
@@ -4,7 +4,7 @@
 from jax.sharding import PartitionSpec as P
 
 
-def shards(pair, cotangent, w_left, w_left_gate, w_right, w_right_gate):
+def gathered_shards(pair, cotangent, w_left, w_left_gate, w_right, w_right_gate):
     pair_f = pair.astype(jnp.float32)
     average = jnp.mean(pair_f, axis=-1, keepdims=True)
     centered_input = pair_f - average
@@ -70,7 +70,90 @@
     return (pair_gradient, pieces_w[0], pieces_w[1], pieces_w[2], pieces_w[3])
 
 
+def axis_sum(value, axis, size):
+    if size & (size - 1):
+        return lax.psum(value, axis)
+    step = 1
+    while step < size:
+        pairs = [(i, i ^ step) for i in range(size)]
+        value = value + lax.ppermute(value, axis, pairs)
+        step *= 2
+    return value
+
+
+def channel_shards(sizes, pair, cotangent, w_left, w_left_gate, w_right, w_right_gate):
+    rows, cols = sizes
+    devices = rows * cols
+    hidden, r, c = cotangent.shape
+    own = hidden // devices
+    pair_f = pair.astype(jnp.float32)
+    average = jnp.mean(pair_f, axis=-1, keepdims=True)
+    centered_input = pair_f - average
+    variance = jnp.mean(centered_input * centered_input, axis=-1, keepdims=True)
+    inverse_scale = 1.0 / jnp.sqrt(variance + 1e-05)
+    standardized_input = centered_input * inverse_scale
+    normalized_input = standardized_input.astype(jnp.bfloat16)
+    stacked = jnp.concatenate([w_left, w_left_gate, w_right, w_right_gate], axis=1)
+    projected = jnp.einsum(
+        "rcd,dh->hrc", normalized_input, stacked, preferred_element_type=jnp.float32
+    )
+    q_left, p_left, q_right, p_right = jnp.split(projected, 4, axis=0)
+    s_left = jax.nn.sigmoid(p_left)
+    s_right = jax.nn.sigmoid(p_right)
+    left = (s_left * q_left).astype(jnp.bfloat16)
+    right = (s_right * q_right).astype(jnp.bfloat16)
+
+    def out_of(parts):
+        parts = [p.reshape(devices, own, r, c) for p in parts]
+        sent = jnp.concatenate(parts, axis=1)
+        got = lax.all_to_all(sent, ("row", "col"), split_axis=0, concat_axis=0, tiled=True)
+        got = got.reshape(rows, cols, len(parts), own, r, c)
+        whole = got.transpose(2, 3, 0, 4, 1, 5)
+        return whole.reshape(len(parts), own, rows * r, cols * c)
+
+    def back(parts):
+        whole = jnp.stack(parts, axis=0).reshape(len(parts), own, rows, r, cols, c)
+        sent = whole.transpose(2, 4, 0, 1, 3, 5).reshape(devices, len(parts) * own, r, c)
+        got = lax.all_to_all(sent, ("row", "col"), split_axis=0, concat_axis=0, tiled=True)
+        got = got.reshape(devices, len(parts), own, r, c)
+        return [got[:, i].reshape(hidden, r, c) for i in range(len(parts))]
+
+    g_all, left_all, right_all = out_of([cotangent, left, right])
+    d_left = jnp.einsum("hij,hjk->hik", g_all, right_all, preferred_element_type=jnp.float32)
+    d_right = jnp.einsum("hij,hik->hjk", g_all, left_all, preferred_element_type=jnp.float32)
+    d_left_tile, d_right_tile = back([d_left.astype(jnp.bfloat16), d_right.astype(jnp.bfloat16)])
+    grad_l = d_left_tile.astype(jnp.float32)
+    grad_r = d_right_tile.astype(jnp.float32)
+    e_left = grad_l * s_left
+    f_left = grad_l * q_left * s_left * (1.0 - s_left)
+    e_right = grad_r * s_right
+    f_right = grad_r * q_right * s_right * (1.0 - s_right)
+    grads = jnp.concatenate([e_left, f_left, e_right, f_right], axis=0).astype(jnp.bfloat16)
+    local_weights = jnp.einsum(
+        "rcd,hrc->dh", normalized_input, grads, preferred_element_type=jnp.float32
+    )
+    total_weights = axis_sum(axis_sum(local_weights, "col", cols), "row", rows) / (rows * r)
+    normalized_gradient = jnp.einsum(
+        "hrc,dh->rcd", grads, stacked, preferred_element_type=jnp.float32
+    )
+    gradient_mean = jnp.mean(normalized_gradient, axis=-1, keepdims=True)
+    gradient_input_mean = jnp.mean(normalized_gradient * standardized_input, axis=-1, keepdims=True)
+    pair_gradient = (
+        (normalized_gradient - gradient_mean - standardized_input * gradient_input_mean)
+        * inverse_scale
+    ).astype(jnp.bfloat16)
+    pieces_w = jnp.split(total_weights, 4, axis=1)
+    return (pair_gradient, pieces_w[0], pieces_w[1], pieces_w[2], pieces_w[3])
+
+
 def solution(mesh):
     in_specs = (P("row", "col", None), P(None, "row", "col"), P(), P(), P(), P())
     out_specs = (P("row", "col", None), P(), P(), P(), P())
+    sizes = (mesh.shape["row"], mesh.shape["col"])
+
+    def shards(pair, cotangent, *weights):
+        if cotangent.shape[0] % (sizes[0] * sizes[1]) == 0:
+            return channel_shards(sizes, pair, cotangent, *weights)
+        return gathered_shards(pair, cotangent, *weights)
+
     return jax.shard_map(shards, mesh=mesh, in_specs=in_specs, out_specs=out_specs, check_vma=False)

time: 587 us -> 206 us (0.35)
  waiting for transfers between devices: 283 us -> 12.2 us
  local copies, waits for them, and re-layouts: 106 us -> 34 us
  matrix products: 26.8 us -> 8.37 us
  between operations: 14.4 us -> 0.92 us
  starting transfers between devices: 0.33 us -> 6.3 us
    all_gather x2 -> x0, waiting for transfers between devices: 172 us -> none  [the longest x1 107 us: shards(): lax.all_gather(right_chan, 'row', axis=1, tiled=True)]
    psum x1 -> x0, waiting for transfers between devices: 111 us -> none  [shards(): total_weights = lax.psum(local_weights, ('row', 'col')) / residues]
    unnamed x30 -> x26, local copies, waits for them, and re-layouts: 46 us -> 13.4 us
    all_to_all x9 -> x0, local copies, waits for them, and re-layouts: 30.2 us -> none  [the longest x2 12.8 us: shards(): lax.all_to_all(g_chan, 'row', split_axis=2, concat_axis=1, tiled=True)]
    convert_element_type x6 -> x0, local copies, waits for them, and re-layouts: 29.7 us -> none  [the longest x1 7.2 us: shards(): d_left.astype(jnp.bfloat16)]
    another operation x0 -> x11, local copies, waits for them, and re-layouts: none -> 19 us  [the longest x7 11.9 us: channel_shards(): g_all, left_all, right_all = out_of([cotangent, left, right])]
    dot_general x5, matrix products: 26.8 us -> 8.37 us  [the longest x1 2.44 us: channel_shards(): jnp.einsum('hij,hik->hjk', g_all, left_all, preferred_element_type=jnp.fl...]
    ppermute x0 -> x5, waiting for transfers between devices: none -> 12.2 us  [axis_sum(): value = value + lax.ppermute(value, axis, pairs)]
  transfers between devices with their start and end apart: 3 -> 5, of which waited for: 3 -> 3; matrix products, arithmetic and copies ran while one was open for 6% -> 4% of each run, Pallas kernels for 0% -> 0%
where the time goes in v1:
time: 206 us
  blocking collectives  130 us (63%)
  local copies, waits for them, and re-layouts  34 us (17%)
  other arithmetic  13.2 us (6%)
  waiting for transfers between devices  12.2 us (6%)
  matrix products  8.37 us (4%)
  starting transfers between devices  6.3 us (3%)
    all_to_all x1, blocking collectives, out_of(): lax.all_to_all(sent, ('row', 'col'), split_axis=0, concat_axis=0, tiled=T...  78.3 us
    all_to_all x1, blocking collectives, back(): lax.all_to_all(sent, ('row', 'col'), split_axis=0, concat_axis=0, tiled=T...  52.2 us
    unnamed x26, local copies, waits for them, and re-layouts  13.4 us
    ppermute x5, waiting for transfers between devices, axis_sum(): value = value + lax.ppermute(value, axis, pairs)  12.2 us
    another operation x7, local copies, waits for them, and re-layouts, channel_shards(): g_all, left_all, right_all = out_of([cotangent, left, right])  11.9 us
    another operation x4, local copies, waits for them, and re-layouts, back(): whole = jnp.stack(parts, axis=0).reshape(len(parts), own, rows, r, cols, c)  7.12 us
    ppermute x5, starting transfers between devices, axis_sum(): value = value + lax.ppermute(value, axis, pairs)  6.3 us
    another operation x1, other arithmetic  5.32 us
  transfers between devices with their start and end apart: 5, of which 3 were waited for; matrix products, arithmetic and copies ran while one was open for 4% of the time, Pallas kernels for 0%

profile of v1, /device:TPU:0, one launch (start us, length us, event | category | flops | bytes accessed | tf_op | source)
XLA Modules:
  0.0 205.5 jit_solution(13048755940660763988)
XLA Ops:
  0.6 3.3 %copy.22 = bf16[32,256,128]{1,2,0:T(8,128)(2,1)S(1)} copy(bf16[32,256,128]{2,1,0:T(8,128)(2,1)} %param.6) | data formatting | bytes 4194304 | tf_op args[0]
  3.9 0.0 copy-start.4
  4.0 0.4 convert_reduce_fusion
  4.3 0.7 fusion.9
  5.1 1.3 fusion.18
  6.4 1.2 multiply_convert_fusion.5
  7.6 2.0 copy-done
  9.6 0.6 copy.43
  10.2 0.6 copy.44
  10.8 0.0 copy-done.3
  10.8 0.3 pad_maximum_fusion.1
  11.2 78.3 %all_to_all.10 = bf16[32,6,32,256]{3,2,1,0:T(8,128)(2,1)S(1)} all-to-all(bf16[32,6,32,256]{3,2,1,0:T(8,128)(2,1)S(1)} %pad_maximum_fusion.1), channel_id=1, replica_groups=mesh['row'=16,'col'=2] {'row','col'}, dimensions={0} | all-to-all | bytes 6291456 | tf_op jit(solution)/shard_map/all_to_all | solution.py:109
  89.5 1.7 fusion.28
  91.2 1.1 copy.27
  92.2 1.5 unstack.21
  93.8 2.3 %copy.28 = bf16[1,2,16,32,2,256]{5,4,3,2,1,0:T(2,128)(2,1)S(1)} copy(bf16[1,2,16,32,2,256]{5,3,1,0,4,2:T(8,128)(2,1)} %get-tuple-element.26) | data formatting | bytes 2097152 | tf_op jit(solution)/shard_map/unstack | solution.py:121
  96.1 1.5 unstack.23
  97.6 2.3 %copy.26 = bf16[1,2,16,32,2,256]{5,4,3,2,1,0:T(2,128)(2,1)S(1)} copy(bf16[1,2,16,32,2,256]{5,3,1,0,4,2:T(8,128)(2,1)} %get-tuple-element.27) | data formatting | bytes 2097152 | tf_op jit(solution)/shard_map/unstack | solution.py:121
  99.9 1.5 unstack.19
  101.4 2.4 %convolution_convert_fusion = bf16[2,512,512]{2,1,0:T(8,128)(2,1)S(1)} fusion(bf16[2,512,512]{2,1,0:T(8,128)(2,1)} %unstack.19, bf16[2,512,512]{2,1,0:T(8,128)(2,1)} %unstack.23), kind=kOutput, calls=%fused_computation.31 | convolution fusion | flops 537395200 | bytes 3145728 | tf_op jit(solution)/shard_map/hij,hik->hjk/dot_general | solution.py:123
  103.8 1.7 convolution_convert_fusion.1
  105.5 2.2 %stack.9 = bf16[1,2,16,32,2,256]{5,4,3,2,1,0:T(2,128)(2,1)} reshape(bf16[2,512,512]{2,1,0:T(8,128)(2,1)} %convolution_convert_fusion.1) | data formatting | bytes 2097152 | tf_op jit(solution)/shard_map/stack | solution.py:115
  107.8 2.4 %copy.30 = bf16[1,2,16,32,2,256]{5,3,1,0,4,2:T(8,128)(2,1)} copy(bf16[1,2,16,32,2,256]{5,4,3,2,1,0:T(2,128)(2,1)} %stack.9) | data formatting | bytes 2097152 | tf_op jit(solution)/shard_map/stack | solution.py:115
  110.1 1.1 stack.10
  111.2 1.4 copy.31
  112.7 1.6 pad_maximum_fusion.2
  114.3 52.2 %all_to_all.11 = bf16[32,4,32,256]{3,2,1,0:T(8,128)(2,1)S(1)} all-to-all(bf16[32,4,32,256]{3,2,1,0:T(8,128)(2,1)S(1)} %bitcast.33), channel_id=1, replica_groups=mesh['row'=16,'col'=2] {'row','col'}, dimensions={0} | all-to-all | bytes 4194304 | tf_op jit(solution)/shard_map/all_to_all | solution.py:117
  166.4 0.3 fusion.29
  166.7 0.6 bitcast_convert_fusion
  167.4 1.2 slice-done.1
  168.6 5.3 %multiply_convert_fusion.3 = (bf16[64,32,256]{2,0,1:T(8,128)(2,1)S(1)}, bf16[64,32,256]{2,0,1:T(8,128)(2,1)S(1)}, bf16[64,32,256]{2,0,1:T(8,128)(2,1)S(1)}, bf16[64,32,256]{2,0,1:T(8,128)(2,1)S(1)}) fusion(f32[64,32,256]{2,1,0:T(8,128)S(1)} %get-tuple-element.36, f32[256,32,256]{2,0,1:T(8,128)S(1)} %bitcast.30, f32[64,32,256]{2,1,0:T(8,128)S(1)} %get-tuple-element.35), kind=kLoop, calls=%fused_computation.26 | loop fusion | flops 10485760 | bytes 16777216 | tf_op jit(solution)/shard_map/convert.2
  173.9 1.5 fusion.20
  175.5 1.5 collective-permute-start
  177.0 3.9 %collective-permute-done = f32[128,256]{1,0:T(8,128)S(1)} collective-permute-done((f32[128,256]{1,0:T(8,128)S(1)}, f32[128,256]{1,0:T(8,128)S(1)}, u32[]{:S(2)}, u32[]{:S(2)}) %collective-permute-start) | collective-permute-done | bytes 131104 | tf_op jit(solution)/shard_map/ppermute | solution.py:79
  181.0 0.1 collective-permute-start.1
  181.0 1.4 fusion.27
  182.5 1.9 collective-permute-start.2
  184.4 4.1 %collective-permute-done.2 = f32[128,256]{1,0:T(8,128)S(1)} collective-permute-done((f32[128,256]{1,0:T(8,128)S(1)}, f32[128,256]{1,0:T(8,128)S(1)}, u32[]{:S(2)}, u32[]{:S(2)}) %collective-permute-start.2) | collective-permute-done | bytes 131104 | tf_op jit(solution)/shard_map/ppermute | solution.py:79
  188.6 1.2 collective-permute-start.3
  189.8 4.1 %collective-permute-done.3 = f32[128,256]{1,0:T(8,128)S(1)} collective-permute-done((f32[128,256]{1,0:T(8,128)S(1)}, f32[128,256]{1,0:T(8,128)S(1)}, u32[]{:S(2)}, u32[]{:S(2)}) %collective-permute-start.3) | collective-permute-done | bytes 131104 | tf_op jit(solution)/shard_map/ppermute | solution.py:79
  193.9 1.6 collective-permute-start.4
  195.5 3.0 %fusion.8 = bf16[32,256,128]{1,2,0:T(8,128)(2,1)} fusion(bf16[32,256,128]{1,2,0:T(8,128)(2,1)S(1)} %copy.22, f32[32,256,128]{1,2,0:T(8,128)S(1)} %get-tuple-element.34, f32[32,256]{1,0:T(8,128)S(1)} %broadcast_multiply_fusion, f32[32,256]{1,0:T(8,128)S(1)} %broadcast_multiply_fusion.1, f32[32,256]{1,0:T(8,128)S(1)} %add_rsqrt_fusion, ...), kind=kLoop, calls=%fused_computation.10 | loop fusion | flops 8388608 | bytes 8519680 | tf_op jit(solution)/shard_map/convert_element_type | solution.py:144
  198.5 4.1 %copy.35 = bf16[32,256,128]{2,1,0:T(8,128)(2,1)} copy(bf16[32,256,128]{1,2,0:T(8,128)(2,1)} %fusion.8) | data formatting | bytes 4194304
  202.6 0.1 fusion.30
  202.7 0.7 copy.39
  203.4 0.7 copy.38
  204.1 0.7 copy.37
  204.8 0.7 copy.36
  (28 shorter events, 0.2 us)
Async XLA Ops:
  3.9 1.1 copy-start.4
  3.9 1.1 copy-start.5
  3.9 1.1 copy-start.6
  3.9 1.1 copy-start.7
  6.4 3.2 %copy-start = (f32[256,32,256]{2,0,1:T(8,128)}, f32[256,32,256]{2,0,1:T(8,128)S(1)}, u32[]{:S(2)}) copy-start(f32[256,32,256]{2,0,1:T(8,128)S(1)} %fusion.18) | copy-start | bytes 25165828
  9.6 1.2 copy-start.3
  101.4 2.5 %copy-start.1 = (bf16[2,512,512]{2,1,0:T(8,128)(2,1)S(1)}, bf16[2,512,512]{2,1,0:T(8,128)(2,1)}, u32[]{:S(2)}) copy-start(bf16[2,512,512]{2,1,0:T(8,128)(2,1)} %unstack.19) | copy-start | bytes 3145732
  101.4 2.5 %copy-start.2 = (bf16[2,512,512]{2,1,0:T(8,128)(2,1)S(1)}, bf16[2,512,512]{2,1,0:T(8,128)(2,1)}, u32[]{:S(2)}) copy-start(bf16[2,512,512]{2,1,0:T(8,128)(2,1)} %unstack.21) | copy-start | bytes 3145732
  112.7 54.7 %slice-start = ((s8[8388608]{0:T(1024)(128)(4,1)}), s8[4194304]{0:T(1024)(128)(4,1)S(1)}, s32[]{:S(2)}) async-start(s8[8388608]{0:T(1024)(128)(4,1)} %bitcast.29), calls=%async_computation.2 | async-start | bytes 8388608
  166.4 2.2 %slice-start.1 = ((s8[8388608]{0:T(1024)(128)(4,1)}), s8[4194304]{0:T(1024)(128)(4,1)S(1)}, s32[]{:S(2)}) async-start(s8[8388608]{0:T(1024)(128)(4,1)} %bitcast.29), calls=%async_computation.3 | async-start | bytes 8388608
  175.5 5.5 %collective-permute-start = (f32[128,256]{1,0:T(8,128)S(1)}, f32[128,256]{1,0:T(8,128)S(1)}, u32[]{:S(2)}, u32[]{:S(2)}) collective-permute-start(f32[128,256]{1,0:T(8,128)S(1)} %fusion.20), channel_id=1, source_target_pairs={{0,1},{1,0},{2,3},{3,2},{4,5},{5,4},{6,7},{7,6},{8,9},{9,8},{10,11... | collective-permute-start | bytes 393224 | tf_op jit(solution)/shard_map/ppermute | solution.py:79
  181.0 1.5 collective-permute-start.1
  182.5 6.0 %collective-permute-start.2 = (f32[128,256]{1,0:T(8,128)S(1)}, f32[128,256]{1,0:T(8,128)S(1)}, u32[]{:S(2)}, u32[]{:S(2)}) collective-permute-start(f32[128,256]{1,0:T(8,128)S(1)} %add.37), channel_id=1, source_target_pairs={{0,4},{2,6},{4,0},{6,2},{8,12},{10,14},{12,8},{14,10},{16,20},{18,... | collective-permute-start | bytes 393224 | tf_op jit(solution)/shard_map/ppermute | solution.py:79
  188.6 5.3 %collective-permute-start.3 = (f32[128,256]{1,0:T(8,128)S(1)}, f32[128,256]{1,0:T(8,128)S(1)}, u32[]{:S(2)}, u32[]{:S(2)}) collective-permute-start(f32[128,256]{1,0:T(8,128)S(1)} %add.38), channel_id=1, source_target_pairs={{0,8},{2,10},{4,12},{6,14},{8,0},{10,2},{12,4},{14,6},{16,24},{18,... | collective-permute-start | bytes 393224 | tf_op jit(solution)/shard_map/ppermute | solution.py:79
  193.9 8.7 %collective-permute-start.4 = (f32[128,256]{1,0:T(8,128)S(1)}, f32[128,256]{1,0:T(8,128)S(1)}, u32[]{:S(2)}, u32[]{:S(2)}) collective-permute-start(f32[128,256]{1,0:T(8,128)S(1)} %add.39), channel_id=1, source_target_pairs={{0,16},{2,18},{4,20},{6,22},{8,24},{10,26},{12,28},{14,30},{16,0},... | collective-permute-start | bytes 393224 | tf_op jit(solution)/shard_map/ppermute | solution.py:79

commit v2 on v0

--- a/solution.py
+++ b/solution.py
@@ -1,10 +1,16 @@
+import functools
+
 import jax
 import jax.numpy as jnp
 from jax import lax
+from jax.experimental import pallas as pl
+from jax.experimental.pallas import tpu as pltpu
 from jax.sharding import PartitionSpec as P
 
-
-def shards(pair, cotangent, w_left, w_left_gate, w_right, w_right_gate):
+BF16, F32 = jnp.bfloat16, jnp.float32
+
+
+def gathered_shards(pair, cotangent, w_left, w_left_gate, w_right, w_right_gate):
     pair_f = pair.astype(jnp.float32)
     average = jnp.mean(pair_f, axis=-1, keepdims=True)
     centered_input = pair_f - average
@@ -70,7 +76,204 @@
     return (pair_gradient, pieces_w[0], pieces_w[1], pieces_w[2], pieces_w[3])
 
 
+NT = (((1,), (1,)), ((), ()))
+TN = (((0,), (0,)), ((), ()))
+NN = (((1,), (0,)), ((), ()))
+
+
+def stack_weights(w_refs, wt_ref):
+    h = w_refs[0].shape[1]
+    for i, w_ref in enumerate(w_refs):
+        wt_ref[pl.ds(i * h, h), :] = w_ref[...].astype(F32).T.astype(BF16)
+
+
+def layer_norm(x):
+    x = x.astype(F32)
+    centered = x - jnp.mean(x, axis=-1, keepdims=True)
+    variance = jnp.mean(centered * centered, axis=-1, keepdims=True)
+    inverse_scale = lax.rsqrt(variance + 1e-05)
+    return centered * inverse_scale, inverse_scale
+
+
+def project(wt_ref, normed):
+    projected = lax.dot_general(wt_ref[...], normed, NT, preferred_element_type=F32)
+    h = projected.shape[0] // 4
+    q_left, p_left, q_right, p_right = (projected[i * h : (i + 1) * h] for i in range(4))
+    return q_left, jax.nn.sigmoid(p_left), q_right, jax.nn.sigmoid(p_right)
+
+
+def put_lanes(ref, at, value):
+    lanes = ref.shape[2]
+    for i in range(ref.shape[0]):
+        ref[i, at, :] = value[:, i * lanes : (i + 1) * lanes]
+
+
+def get_lanes(ref, at):
+    return jnp.concatenate([ref[i, at, :] for i in range(ref.shape[0])], axis=1)
+
+
+def before_kernel(own, pair_ref, cot_ref, wl, wlg, wr, wrg, out_ref, wt_ref, rows_ref):
+    stack_weights((wl, wlg, wr, wrg), wt_ref)
+    h = wl.shape[1]
+    rows = pair_ref.shape[0]
+
+    def one_row(r, carry):
+        normed, _ = layer_norm(pair_ref[r])
+        q_left, s_left, q_right, s_right = project(wt_ref, normed.astype(BF16))
+        start = pl.multiple_of(r * 2 * h, 2 * h)
+        put_lanes(rows_ref, pl.ds(start, h), s_left * q_left)
+        put_lanes(rows_ref, pl.ds(start + h, h), s_right * q_right)
+        return carry
+
+    lax.fori_loop(0, rows, one_row, 0, unroll=2)
+    for channel in range(h):
+        to, slot = channel // own, (channel % own) * 3
+        out_ref[to, slot] = cot_ref[channel]
+        for side in range(2):
+            line = get_lanes(rows_ref, pl.ds(side * h + channel, rows, stride=2 * h))
+            out_ref[to, slot + 1 + side] = line.astype(BF16)
+
+
+def triangle_kernel(rows, cols, in_ref, out_ref, g_ref, l_ref, r_ref):
+    r, c = in_ref.shape[2:]
+    for a in range(rows):
+        for b in range(cols):
+            for i, ref in enumerate((g_ref, l_ref, r_ref)):
+                ref[pl.ds(a * r, r), pl.ds(b * c, c)] = in_ref[a * cols + b, i]
+    for i, (dims, ref) in enumerate(((NN, r_ref), (TN, l_ref))):
+        d = lax.dot_general(g_ref[...], ref[...], dims, preferred_element_type=F32).astype(BF16)
+        for a in range(rows):
+            for b in range(cols):
+                out_ref[a * cols + b, i] = d[a * r : (a + 1) * r, b * c : (b + 1) * c]
+
+
+def after_kernel(own, pair_ref, d_ref, wl, wlg, wr, wrg, out_ref, grad_ref, wt_ref, rows_ref):
+    stack_weights((wl, wlg, wr, wrg), wt_ref)
+    h = wl.shape[1]
+    rows = pair_ref.shape[0]
+
+    @pl.when(pl.program_id(0) == 0)
+    def _():
+        grad_ref[...] = jnp.zeros_like(grad_ref)
+
+    for channel in range(h):
+        to, slot = channel // own, (channel % own) * 2
+        for side in range(2):
+            line = d_ref[to, slot + side].astype(F32)
+            put_lanes(rows_ref, pl.ds(side * h + channel, rows, stride=2 * h), line)
+
+    def one_row(r, carry):
+        standardized, inverse_scale = layer_norm(pair_ref[r])
+        normed = standardized.astype(BF16)
+        q_left, s_left, q_right, s_right = project(wt_ref, normed)
+        start = pl.multiple_of(r * 2 * h, 2 * h)
+        e_left = get_lanes(rows_ref, pl.ds(start, h)) * s_left
+        e_right = get_lanes(rows_ref, pl.ds(start + h, h)) * s_right
+        f_left = e_left * q_left * (1.0 - s_left)
+        f_right = e_right * q_right * (1.0 - s_right)
+        grads = jnp.concatenate([e_left, f_left, e_right, f_right], axis=0).astype(BF16)
+        grad_ref[...] += lax.dot_general(grads, normed, NN, preferred_element_type=F32)
+        d_normed = lax.dot_general(grads, wt_ref[...], TN, preferred_element_type=F32)
+        mean = jnp.mean(d_normed, axis=-1, keepdims=True)
+        input_mean = jnp.mean(d_normed * standardized, axis=-1, keepdims=True)
+        out_ref[r] = ((d_normed - mean - standardized * input_mean) * inverse_scale).astype(BF16)
+        return carry
+
+    lax.fori_loop(0, rows, one_row, 0, unroll=2)
+
+
+def share_kernel(scale, in_ref, out_ref):
+    total = jnp.sum(in_ref[...], axis=0, keepdims=True) * scale
+    out_ref[...] = jnp.broadcast_to(total, out_ref.shape)
+
+
+def weights_kernel(in_ref, *out_refs):
+    total = in_ref[...].T
+    h = total.shape[1] // 4
+    for i, out_ref in enumerate(out_refs):
+        out_ref[...] = total[:, i * h : (i + 1) * h]
+
+
+def channel_shards(sizes, pair, cotangent, *weights):
+    rows, cols = sizes
+    devices = rows * cols
+    hidden, r, c = cotangent.shape
+    dim = pair.shape[2]
+    own = hidden // devices
+    block = 16 if r % 16 == 0 else r
+    grid = (r // block,)
+    params = pltpu.CompilerParams(vmem_limit_bytes=48 * 2**20)
+    whole = pl.BlockSpec(weights[0].shape, lambda i: (0, 0))
+    tile = pl.BlockSpec((block, c, dim), lambda i: (i, 0, 0))
+    exchange = functools.partial(
+        lax.all_to_all, axis_name=("row", "col"), split_axis=0, concat_axis=0, tiled=True
+    )
+    lanes = min(c, 128)
+    scratch = [
+        pltpu.VMEM((4 * hidden, dim), BF16),
+        pltpu.VMEM((c // lanes, 2 * hidden * block, lanes), F32),
+    ]
+
+    sent = pl.pallas_call(
+        functools.partial(before_kernel, own),
+        grid=grid,
+        in_specs=[tile, pl.BlockSpec((hidden, block, c), lambda i: (0, i, 0))] + [whole] * 4,
+        out_specs=pl.BlockSpec((devices, 3 * own, block, c), lambda i: (0, 0, i, 0)),
+        out_shape=jax.ShapeDtypeStruct((devices, 3 * own, r, c), BF16),
+        scratch_shapes=scratch,
+        compiler_params=params,
+        name="before",
+    )(pair, cotangent, *weights)
+
+    n_i, n_k = rows * r, cols * c
+    sent = pl.pallas_call(
+        functools.partial(triangle_kernel, rows, cols),
+        grid=(own,),
+        in_specs=[pl.BlockSpec((devices, 3, r, c), lambda i: (0, i, 0, 0))],
+        out_specs=pl.BlockSpec((devices, 2, r, c), lambda i: (0, i, 0, 0)),
+        out_shape=jax.ShapeDtypeStruct((devices, 2 * own, r, c), BF16),
+        scratch_shapes=[pltpu.VMEM((n_i, n_k), BF16)] * 3,
+        compiler_params=params,
+        name="triangle",
+    )(exchange(sent))
+
+    pair_gradient, local_weights = pl.pallas_call(
+        functools.partial(after_kernel, own),
+        grid=grid,
+        in_specs=[tile, pl.BlockSpec((devices, 2 * own, block, c), lambda i: (0, 0, i, 0))]
+        + [whole] * 4,
+        out_specs=[tile, pl.BlockSpec((4 * hidden, dim), lambda i: (0, 0))],
+        out_shape=[
+            jax.ShapeDtypeStruct(pair.shape, BF16),
+            jax.ShapeDtypeStruct((4 * hidden, dim), F32),
+        ],
+        scratch_shapes=scratch,
+        compiler_params=params,
+        name="after",
+    )(pair, exchange(sent), *weights)
+
+    blocks = exchange(local_weights.reshape(devices, 4 * own, dim))
+    shared = pl.pallas_call(
+        functools.partial(share_kernel, 1.0 / n_i),
+        out_shape=jax.ShapeDtypeStruct(blocks.shape, F32),
+        name="share",
+    )(blocks)
+    grads = pl.pallas_call(
+        weights_kernel,
+        out_shape=[jax.ShapeDtypeStruct((dim, hidden), F32)] * 4,
+        name="weights",
+    )(exchange(shared).reshape(4 * hidden, dim))
+    return (pair_gradient, *grads)
+
+
 def solution(mesh):
     in_specs = (P("row", "col", None), P(None, "row", "col"), P(), P(), P(), P())
     out_specs = (P("row", "col", None), P(), P(), P(), P())
+    sizes = (mesh.shape["row"], mesh.shape["col"])
+
+    def shards(pair, cotangent, *weights):
+        if cotangent.shape[0] % (sizes[0] * sizes[1]) == 0:
+            return channel_shards(sizes, pair, cotangent, *weights)
+        return gathered_shards(pair, cotangent, *weights)
+
     return jax.shard_map(shards, mesh=mesh, in_specs=in_specs, out_specs=out_specs, check_vma=False)

time: 587 us -> 203 us (0.35)
  waiting for transfers between devices: 283 us -> 0 us
  local copies, waits for them, and re-layouts: 106 us -> 12.3 us
  Pallas kernels: 0 us -> 34.8 us
  matrix products: 26.8 us -> 0 us
  blocking collectives: 135 us -> 155 us
  other arithmetic: 16.7 us -> 0 us
  between operations: 14.4 us -> 0.67 us
    all_gather x2 -> x0, waiting for transfers between devices: 172 us -> none  [the longest x1 107 us: shards(): lax.all_gather(right_chan, 'row', axis=1, tiled=True)]
    psum x1 -> x0, waiting for transfers between devices: 111 us -> none  [shards(): total_weights = lax.psum(local_weights, ('row', 'col')) / residues]
    pallas_call x0 -> x5, Pallas kernels: none -> 34.8 us  [the longest x1 18.7 us: channel_shards(): pl.pallas_call(functools.partial(after_kernel, own), grid=grid, in_specs=...]
    unnamed x30 -> x14, local copies, waits for them, and re-layouts: 46 us -> 12.3 us
    all_to_all x9 -> x0, local copies, waits for them, and re-layouts: 30.2 us -> none  [the longest x2 12.8 us: shards(): lax.all_to_all(g_chan, 'row', split_axis=2, concat_axis=1, tiled=True)]
    convert_element_type x6 -> x0, local copies, waits for them, and re-layouts: 29.7 us -> none  [the longest x1 7.2 us: shards(): d_left.astype(jnp.bfloat16)]
    dot_general x5 -> x0, matrix products: 26.8 us -> none  [the longest x1 9.61 us: shards(): jnp.einsum('hij,hjk->hik', g_chan, lax.all_gather(right_chan, 'row', axis...]
    all_to_all x6 -> x4, blocking collectives: 135 us -> 155 us  [the longest x2 131 us: channel_shards(): exchange(sent)]
  transfers between devices with their start and end apart: 3 -> 0, of which waited for: 3 -> 0; matrix products, arithmetic and copies ran while one was open for 6% -> 0% of each run, Pallas kernels for 0% -> 0%
where the time goes in v2:
time: 203 us
  blocking collectives  155 us (76%)
  Pallas kernels  34.8 us (17%)
  local copies, waits for them, and re-layouts  12.3 us (6%)
    all_to_all x2, blocking collectives, channel_shards(): exchange(sent)  131 us
    pallas_call x1, Pallas kernels, channel_shards(): pl.pallas_call(functools.partial(after_kernel, own), grid=grid, in_specs=...  18.7 us
    unnamed x14, local copies, waits for them, and re-layouts  12.3 us
    all_to_all x1, blocking collectives, channel_shards(): blocks = exchange(local_weights.reshape(devices, 4 * own, dim))  12.2 us
    all_to_all x1, blocking collectives, channel_shards(): exchange(shared).reshape(4 * hidden, dim)  11.9 us
    pallas_call x1, Pallas kernels, channel_shards(): pl.pallas_call(functools.partial(before_kernel, own), grid=grid, in_specs...  10.9 us

profile of v2, /device:TPU:0, one launch (start us, length us, event | category | flops | bytes accessed | tf_op | source)
XLA Modules:
  0.0 202.5 jit_solution(8211573079296063567)
XLA Ops:
  0.6 0.8 copy.11.wl
  1.5 0.8 copy.12.wlg
  2.3 0.8 copy.13.wr
  3.1 0.8 copy.14.wrg
  4.0 0.0 copy-start
  4.0 1.6 copy-done
  5.6 0.0 copy-start.2
  5.6 1.2 copy-done.2
  6.8 10.9 %before.1 = bf16[32,6,32,256]{3,2,1,0:T(8,128)(2,1)} custom-call(bf16[32,256,128]{2,1,0:T(8,128)(2,1)S(1)} %copy-done, bf16[64,32,256]{2,1,0:T(8,128)(2,1)S(1)} %copy-done.2, bf16[128,64]{1,0:T(8,128)(2,1)S(1)} %copy.11.wl, bf16[128,64]{1,0:T(8,128)(2,1)S(1)} %copy.12.wlg, bf16[128,64]{1,0:T(8,128)(2,1)S(1)} %copy.13.wr, bf16[128,64]{1,0:T(8,128)(2,1)S(1)} %copy.14.wrg), custom_call_target="tpu_custom_call" | custom-call | tf_op jit(solution)/shard_map/before/pallas_call | solution.py:217
  17.7 78.5 %all_to_all.20.in_ref = bf16[32,6,32,256]{3,2,1,0:T(8,128)(2,1)S(1)} all-to-all(bf16[32,6,32,256]{3,2,1,0:T(8,128)(2,1)} %before.1), channel_id=1, replica_groups=mesh['row'=16,'col'=2] {'row','col'}, dimensions={0} | all-to-all | bytes 6291456 | tf_op jit(solution)/shard_map/all_to_all | solution.py:238
  96.2 1.8 triangle.1
  98.0 0.0 copy-start.1
  98.0 52.2 %all_to_all.21.d_ref = bf16[32,4,32,256]{3,2,1,0:T(8,128)(2,1)S(1)} all-to-all(bf16[32,4,32,256]{3,2,1,0:T(8,128)(2,1)S(1)} %triangle.1), channel_id=1, replica_groups=mesh['row'=16,'col'=2] {'row','col'}, dimensions={0} | all-to-all | bytes 4194304 | tf_op jit(solution)/shard_map/all_to_all | solution.py:253
  150.2 0.0 copy-done.1
  150.2 18.7 %after.1 = (bf16[32,256,128]{2,1,0:T(8,128)(2,1)}, f32[256,128]{1,0:T(8,128)S(1)}) custom-call(bf16[32,256,128]{2,1,0:T(8,128)(2,1)S(1)} %copy-done.1, bf16[32,4,32,256]{3,2,1,0:T(8,128)(2,1)S(1)} %all_to_all.21.d_ref, bf16[128,64]{1,0:T(8,128)(2,1)S(1)} %copy.11.wl, bf16[128,64]{1,0:T(8,128)(2,1)S(1)} %copy.12.wlg, bf16[128,64]{1,0:T(8,128)(2,1)S(1)} %copy.13.wr, ...), custom_call_target="tpu_custom_call" | custom-call | tf_op jit(solution)/shard_map/after/pallas_call | solution.py:240
  169.0 12.2 %all_to_all.22.in_ref = f32[32,8,128]{2,1,0:T(8,128)} all-to-all(f32[32,8,128]{2,1,0:T(8,128)S(1)} %bitcast.2), channel_id=1, replica_groups=mesh['row'=16,'col'=2] {'row','col'}, dimensions={0} | all-to-all | bytes 262144 | tf_op jit(solution)/shard_map/all_to_all | solution.py:255
  181.2 1.6 share.1
  182.8 11.9 %all_to_all.23 = f32[32,8,128]{2,1,0:T(8,128)} all-to-all(f32[32,8,128]{2,1,0:T(8,128)} %share.1), channel_id=1, replica_groups=mesh['row'=16,'col'=2] {'row','col'}, dimensions={0} | all-to-all | bytes 262144 | tf_op jit(solution)/shard_map/all_to_all | solution.py:265
  194.6 1.7 weights.1
  196.4 1.5 copy.19
  197.9 1.5 copy.20
  199.5 1.5 copy.21
  201.0 1.5 copy.22
Async XLA Ops:
  4.0 1.6 copy-start
  5.6 1.2 copy-start.2
  98.0 52.2 %copy-start.1 = (bf16[32,256,128]{2,1,0:T(8,128)(2,1)S(1)}, bf16[32,256,128]{2,1,0:T(8,128)(2,1)}, u32[]{:S(2)}) copy-start(bf16[32,256,128]{2,1,0:T(8,128)(2,1)} %pair_ref.3) | copy-start | bytes 6291460

commit v3 on v2

--- a/solution.py
+++ b/solution.py
@@ -81,22 +81,26 @@
 NN = (((1,), (0,)), ((), ()))
 
 
-def stack_weights(w_refs, wt_ref):
-    h = w_refs[0].shape[1]
-    for i, w_ref in enumerate(w_refs):
-        wt_ref[pl.ds(i * h, h), :] = w_ref[...].astype(F32).T.astype(BF16)
+def dot(a, b, dims=NN):
+    return lax.dot_general(a, b, dims, preferred_element_type=F32)
+
+
+def stack_weights(w_refs, w_ref):
+    h = w_refs[0].shape[0]
+    for i, ref in enumerate(w_refs):
+        w_ref[pl.ds(i * h, h), :] = ref[...]
 
 
 def layer_norm(x):
-    x = x.astype(F32)
-    centered = x - jnp.mean(x, axis=-1, keepdims=True)
-    variance = jnp.mean(centered * centered, axis=-1, keepdims=True)
+    x = x.T.astype(F32)
+    centered = x - jnp.mean(x, axis=0, keepdims=True)
+    variance = jnp.mean(centered * centered, axis=0, keepdims=True)
     inverse_scale = lax.rsqrt(variance + 1e-05)
     return centered * inverse_scale, inverse_scale
 
 
-def project(wt_ref, normed):
-    projected = lax.dot_general(wt_ref[...], normed, NT, preferred_element_type=F32)
+def project(w_ref, normed):
+    projected = dot(w_ref[...], normed)
     h = projected.shape[0] // 4
     q_left, p_left, q_right, p_right = (projected[i * h : (i + 1) * h] for i in range(4))
     return q_left, jax.nn.sigmoid(p_left), q_right, jax.nn.sigmoid(p_right)
@@ -112,20 +116,20 @@
     return jnp.concatenate([ref[i, at, :] for i in range(ref.shape[0])], axis=1)
 
 
-def before_kernel(own, pair_ref, cot_ref, wl, wlg, wr, wrg, out_ref, wt_ref, rows_ref):
-    stack_weights((wl, wlg, wr, wrg), wt_ref)
-    h = wl.shape[1]
+def before_kernel(own, pair_ref, cot_ref, wl, wlg, wr, wrg, out_ref, w_ref, rows_ref):
+    stack_weights((wl, wlg, wr, wrg), w_ref)
+    h = wl.shape[0]
     rows = pair_ref.shape[0]
 
     def one_row(r, carry):
         normed, _ = layer_norm(pair_ref[r])
-        q_left, s_left, q_right, s_right = project(wt_ref, normed.astype(BF16))
+        q_left, s_left, q_right, s_right = project(w_ref, normed.astype(BF16))
         start = pl.multiple_of(r * 2 * h, 2 * h)
         put_lanes(rows_ref, pl.ds(start, h), s_left * q_left)
         put_lanes(rows_ref, pl.ds(start + h, h), s_right * q_right)
         return carry
 
-    lax.fori_loop(0, rows, one_row, 0, unroll=2)
+    lax.fori_loop(0, rows, one_row, 0, unroll=4)
     for channel in range(h):
         to, slot = channel // own, (channel % own) * 3
         out_ref[to, slot] = cot_ref[channel]
@@ -141,15 +145,16 @@
             for i, ref in enumerate((g_ref, l_ref, r_ref)):
                 ref[pl.ds(a * r, r), pl.ds(b * c, c)] = in_ref[a * cols + b, i]
     for i, (dims, ref) in enumerate(((NN, r_ref), (TN, l_ref))):
-        d = lax.dot_general(g_ref[...], ref[...], dims, preferred_element_type=F32).astype(BF16)
+        d = dot(g_ref[...], ref[...], dims).astype(BF16)
         for a in range(rows):
             for b in range(cols):
                 out_ref[a * cols + b, i] = d[a * r : (a + 1) * r, b * c : (b + 1) * c]
 
 
-def after_kernel(own, pair_ref, d_ref, wl, wlg, wr, wrg, out_ref, grad_ref, wt_ref, rows_ref):
-    stack_weights((wl, wlg, wr, wrg), wt_ref)
-    h = wl.shape[1]
+def after_kernel(own, pair_ref, d_ref, wl, wlg, wr, wrg, out_ref, grad_ref, w_ref, back_ref, rows_ref):
+    stack_weights((wl, wlg, wr, wrg), w_ref)
+    back_ref[...] = w_ref[...].T
+    h = wl.shape[0]
     rows = pair_ref.shape[0]
 
     @pl.when(pl.program_id(0) == 0)
@@ -165,21 +170,22 @@
     def one_row(r, carry):
         standardized, inverse_scale = layer_norm(pair_ref[r])
         normed = standardized.astype(BF16)
-        q_left, s_left, q_right, s_right = project(wt_ref, normed)
+        q_left, s_left, q_right, s_right = project(w_ref, normed)
         start = pl.multiple_of(r * 2 * h, 2 * h)
         e_left = get_lanes(rows_ref, pl.ds(start, h)) * s_left
         e_right = get_lanes(rows_ref, pl.ds(start + h, h)) * s_right
         f_left = e_left * q_left * (1.0 - s_left)
         f_right = e_right * q_right * (1.0 - s_right)
         grads = jnp.concatenate([e_left, f_left, e_right, f_right], axis=0).astype(BF16)
-        grad_ref[...] += lax.dot_general(grads, normed, NN, preferred_element_type=F32)
-        d_normed = lax.dot_general(grads, wt_ref[...], TN, preferred_element_type=F32)
-        mean = jnp.mean(d_normed, axis=-1, keepdims=True)
-        input_mean = jnp.mean(d_normed * standardized, axis=-1, keepdims=True)
-        out_ref[r] = ((d_normed - mean - standardized * input_mean) * inverse_scale).astype(BF16)
+        grad_ref[...] += dot(grads, normed, NT)
+        d_normed = dot(back_ref[...], grads)
+        mean = jnp.mean(d_normed, axis=0, keepdims=True)
+        input_mean = jnp.mean(d_normed * standardized, axis=0, keepdims=True)
+        moved = (d_normed - mean - standardized * input_mean) * inverse_scale
+        out_ref[r] = moved.astype(BF16).T
         return carry
 
-    lax.fori_loop(0, rows, one_row, 0, unroll=2)
+    lax.fori_loop(0, rows, one_row, 0, unroll=4)
 
 
 def share_kernel(scale, in_ref, out_ref):
@@ -188,10 +194,9 @@
 
 
 def weights_kernel(in_ref, *out_refs):
-    total = in_ref[...].T
-    h = total.shape[1] // 4
+    h = out_refs[0].shape[0]
     for i, out_ref in enumerate(out_refs):
-        out_ref[...] = total[:, i * h : (i + 1) * h]
+        out_ref[...] = in_ref[pl.ds(i * h, h), :]
 
 
 def channel_shards(sizes, pair, cotangent, *weights):
@@ -203,16 +208,15 @@
     block = 16 if r % 16 == 0 else r
     grid = (r // block,)
     params = pltpu.CompilerParams(vmem_limit_bytes=48 * 2**20)
-    whole = pl.BlockSpec(weights[0].shape, lambda i: (0, 0))
+    weights = [w.T for w in weights]
+    whole = pl.BlockSpec((hidden, dim), lambda i: (0, 0))
     tile = pl.BlockSpec((block, c, dim), lambda i: (i, 0, 0))
     exchange = functools.partial(
         lax.all_to_all, axis_name=("row", "col"), split_axis=0, concat_axis=0, tiled=True
     )
     lanes = min(c, 128)
-    scratch = [
-        pltpu.VMEM((4 * hidden, dim), BF16),
-        pltpu.VMEM((c // lanes, 2 * hidden * block, lanes), F32),
-    ]
+    stacked = pltpu.VMEM((4 * hidden, dim), BF16)
+    rows_scratch = pltpu.VMEM((c // lanes, 2 * hidden * block, lanes), F32)
 
     sent = pl.pallas_call(
         functools.partial(before_kernel, own),
@@ -220,7 +224,7 @@
         in_specs=[tile, pl.BlockSpec((hidden, block, c), lambda i: (0, i, 0))] + [whole] * 4,
         out_specs=pl.BlockSpec((devices, 3 * own, block, c), lambda i: (0, 0, i, 0)),
         out_shape=jax.ShapeDtypeStruct((devices, 3 * own, r, c), BF16),
-        scratch_shapes=scratch,
+        scratch_shapes=[stacked, rows_scratch],
         compiler_params=params,
         name="before",
     )(pair, cotangent, *weights)
@@ -247,7 +251,7 @@
             jax.ShapeDtypeStruct(pair.shape, BF16),
             jax.ShapeDtypeStruct((4 * hidden, dim), F32),
         ],
-        scratch_shapes=scratch,
+        scratch_shapes=[stacked, pltpu.VMEM((dim, 4 * hidden), BF16), rows_scratch],
         compiler_params=params,
         name="after",
     )(pair, exchange(sent), *weights)
@@ -260,10 +264,10 @@
     )(blocks)
     grads = pl.pallas_call(
         weights_kernel,
-        out_shape=[jax.ShapeDtypeStruct((dim, hidden), F32)] * 4,
+        out_shape=[jax.ShapeDtypeStruct((hidden, dim), F32)] * 4,
         name="weights",
     )(exchange(shared).reshape(4 * hidden, dim))
-    return (pair_gradient, *grads)
+    return (pair_gradient, *(g.T for g in grads))
 
 
 def solution(mesh):

time: 203 us -> 190 us (0.936)
  local copies, waits for them, and re-layouts: 12.3 us -> 5.71 us
  Pallas kernels: 34.8 us -> 28.4 us
    unnamed x14 -> x22, local copies, waits for them, and re-layouts: 12.3 us -> 5.71 us
    pallas_call x1, Pallas kernels: 10.9 us -> 7.8 us  [channel_shards(): pl.pallas_call(functools.partial(before_kernel, own), grid=grid, in_specs...]
    pallas_call x1, Pallas kernels: 18.7 us -> 15.6 us  [channel_shards(): pl.pallas_call(functools.partial(after_kernel, own), grid=grid, in_specs=...]
where the time goes in v3:
time: 190 us
  blocking collectives  155 us (82%)
  Pallas kernels  28.4 us (15%)
  local copies, waits for them, and re-layouts  5.71 us (3%)
    all_to_all x2, blocking collectives, channel_shards(): exchange(sent)  131 us
    pallas_call x1, Pallas kernels, channel_shards(): pl.pallas_call(functools.partial(after_kernel, own), grid=grid, in_specs=...  15.6 us
    all_to_all x1, blocking collectives, channel_shards(): blocks = exchange(local_weights.reshape(devices, 4 * own, dim))  12.2 us
    all_to_all x1, blocking collectives, channel_shards(): exchange(shared).reshape(4 * hidden, dim)  11.9 us
    pallas_call x1, Pallas kernels, channel_shards(): pl.pallas_call(functools.partial(before_kernel, own), grid=grid, in_specs...  7.8 us
    unnamed x22, local copies, waits for them, and re-layouts  5.71 us

profile of v3, /device:TPU:0, one launch (start us, length us, event | category | flops | bytes accessed | tf_op | source)
XLA Modules:
  0.0 189.5 jit_solution(4843569197641455020)
XLA Ops:
  0.6 0.0 copy-start
  0.6 1.6 copy-done
  2.2 0.0 copy-start.2
  2.2 1.2 copy-done.2
  3.5 0.0 copy-start.3
  3.5 0.7 copy-done.3
  4.2 0.0 copy-start.5
  4.2 0.7 copy-done.5
  4.9 0.0 copy-start.7
  4.9 0.7 copy-done.7
  5.6 0.0 copy-start.9
  5.6 0.7 copy-done.9
  6.3 7.8 %before.1 = bf16[32,6,32,256]{3,2,1,0:T(8,128)(2,1)} custom-call(bf16[32,256,128]{2,1,0:T(8,128)(2,1)S(1)} %copy-done, bf16[64,32,256]{2,1,0:T(8,128)(2,1)S(1)} %copy-done.2, bf16[64,128]{1,0:T(8,128)(2,1)S(1)} %bitcast.11, bf16[64,128]{1,0:T(8,128)(2,1)S(1)} %bitcast.13, bf16[64,128]{1,0:T(8,128)(2,1)S(1)} %bitcast.15, bf16[64,128]{1,0:T(8,128)(2,1)S(1)} %bitcast.17), custom_call_target="tpu_custom_call" | custom-call | tf_op jit(solution)/shard_map/before/pallas_call | solution.py:221
  14.1 78.5 %all_to_all.20.in_ref = bf16[32,6,32,256]{3,2,1,0:T(8,128)(2,1)S(1)} all-to-all(bf16[32,6,32,256]{3,2,1,0:T(8,128)(2,1)} %before.1), channel_id=1, replica_groups=mesh['row'=16,'col'=2] {'row','col'}, dimensions={0} | all-to-all | bytes 6291456 | tf_op jit(solution)/shard_map/all_to_all | solution.py:242
  92.6 1.8 triangle.1
  94.4 0.0 copy-start.1
  94.4 0.0 copy-start.4
  94.4 0.0 copy-start.6
  94.5 0.0 copy-start.8
  94.5 0.0 copy-start.10
  94.5 52.2 %all_to_all.21.d_ref = bf16[32,4,32,256]{3,2,1,0:T(8,128)(2,1)S(1)} all-to-all(bf16[32,4,32,256]{3,2,1,0:T(8,128)(2,1)S(1)} %triangle.1), channel_id=1, replica_groups=mesh['row'=16,'col'=2] {'row','col'}, dimensions={0} | all-to-all | bytes 4194304 | tf_op jit(solution)/shard_map/all_to_all | solution.py:257
  146.6 0.0 copy-done.1
  146.6 0.0 copy-done.4
  146.6 0.0 copy-done.6
  146.7 0.0 copy-done.8
  146.7 0.0 copy-done.10
  146.7 15.6 %after.1 = (bf16[32,256,128]{2,1,0:T(8,128)(2,1)}, f32[256,128]{1,0:T(8,128)S(1)}) custom-call(bf16[32,256,128]{2,1,0:T(8,128)(2,1)S(1)} %copy-done.1, bf16[32,4,32,256]{3,2,1,0:T(8,128)(2,1)S(1)} %all_to_all.21.d_ref, bf16[64,128]{1,0:T(8,128)(2,1)S(1)} %bitcast.12, bf16[64,128]{1,0:T(8,128)(2,1)S(1)} %bitcast.14, bf16[64,128]{1,0:T(8,128)(2,1)S(1)} %bitcast.16, ...), custom_call_target="tpu_custom_call" | custom-call | tf_op jit(solution)/shard_map/after/pallas_call | solution.py:244
  162.3 12.2 %all_to_all.22.in_ref = f32[32,8,128]{2,1,0:T(8,128)} all-to-all(f32[32,8,128]{2,1,0:T(8,128)S(1)} %bitcast.10), channel_id=1, replica_groups=mesh['row'=16,'col'=2] {'row','col'}, dimensions={0} | all-to-all | bytes 262144 | tf_op jit(solution)/shard_map/all_to_all | solution.py:259
  174.5 1.6 share.1
  176.1 11.9 %all_to_all.23 = f32[32,8,128]{2,1,0:T(8,128)} all-to-all(f32[32,8,128]{2,1,0:T(8,128)} %share.1), channel_id=1, replica_groups=mesh['row'=16,'col'=2] {'row','col'}, dimensions={0} | all-to-all | bytes 262144 | tf_op jit(solution)/shard_map/all_to_all | solution.py:269
  188.0 1.6 weights.1
Async XLA Ops:
  0.6 1.6 copy-start
  2.2 1.2 copy-start.2
  3.5 0.7 copy-start.3
  4.2 0.7 copy-start.5
  4.9 0.7 copy-start.7
  5.6 0.7 copy-start.9
  94.4 52.2 %copy-start.1 = (bf16[32,256,128]{2,1,0:T(8,128)(2,1)S(1)}, bf16[32,256,128]{2,1,0:T(8,128)(2,1)}, u32[]{:S(2)}) copy-start(bf16[32,256,128]{2,1,0:T(8,128)(2,1)} %pair_ref.3) | copy-start | bytes 6291460
  94.4 52.2 %copy-start.4 = (bf16[128,64]{0,1:T(8,128)(2,1)S(1)}, bf16[128,64]{0,1:T(8,128)(2,1)}, u32[]{:S(2)}) copy-start(bf16[128,64]{0,1:T(8,128)(2,1)} %param.8) | copy-start | bytes 49156
  94.4 52.2 %copy-start.6 = (bf16[128,64]{0,1:T(8,128)(2,1)S(1)}, bf16[128,64]{0,1:T(8,128)(2,1)}, u32[]{:S(2)}) copy-start(bf16[128,64]{0,1:T(8,128)(2,1)} %param.9) | copy-start | bytes 49156
  94.5 52.2 %copy-start.8 = (bf16[128,64]{0,1:T(8,128)(2,1)S(1)}, bf16[128,64]{0,1:T(8,128)(2,1)}, u32[]{:S(2)}) copy-start(bf16[128,64]{0,1:T(8,128)(2,1)} %param.10) | copy-start | bytes 49156
  94.5 52.2 %copy-start.10 = (bf16[128,64]{0,1:T(8,128)(2,1)S(1)}, bf16[128,64]{0,1:T(8,128)(2,1)}, u32[]{:S(2)}) copy-start(bf16[128,64]{0,1:T(8,128)(2,1)} %param.11) | copy-start | bytes 49156
